TPU v7x, 32 devices: a whole 2x2x4 slice. The times are simulated.
32 devices in a mesh: tx: 4 (over z), ty: 8 (over y, x, core).
Axes of the slice: x: 2, y: 2, z: 4, core: 2. Of those that a mesh axis runs over, the one named last changes fastest.
Arguments:
- object_init: float32 [4, 1024, 2048], P(None, 'tx', 'ty'), may hold values from -5 to 5
- probe: float32 [2, 128, 128], replicated, may hold values from -4 to 4
- propagator_phase: float32 [128, 128], replicated, may hold values from -3.140625 to 3.140625
- measured: bfloat16 [4, 8, 8, 2, 128, 128], P('tx', 'ty'), may hold values from 0 to 1.5
- corners: int32 [4, 8, 16, 2], P('tx', 'ty'), may hold values from 0 to 128
- owner_column: int32 [4, 8, 16, 1], P('tx', 'ty'), may hold values from 0 to 7; in each aligned block of 16 rows (0 to 15, 16 to 31, ..., all dimensions but the last counted through in order) at most 2 rows name the same one
Outputs:
- object_final: float32 [4, 1024, 2048], P(None, 'tx', 'ty')
Inputs may be any that keep to these rules, and one draw needn't show every extreme that they name: `owner_column`: at most 2 of the 16 positions of one tile name the same owner column.
All inputs are finite; a program needn't handle non-finite values.
Results may differ from a plain program's by a relative error of at most 0.0049.
Values may be sent and summed in bfloat16 or wider, within the bound.
A program may use at most 128 MiB of HBM per device.

v0:
```python
import math

import jax
import jax.numpy as jnp
from jax import lax
from jax.sharding import PartitionSpec as P

exact = lax.Precision.HIGHEST
step_rate = 0.5
smooth_rate = 0.2


def padded_2(array, sides, width):
    for axis, dim in sides:
        size, length = (lax.axis_size(axis), array.shape[dim])
        up = [(i, (i + 1) % size) for i in range(size - 1)]
        down = [(j, i) for i, j in up]
        last = lax.slice_in_dim(array, length - width, length, axis=dim)
        leading = lax.slice_in_dim(array, 0, width, axis=dim)
        before = lax.ppermute(last, axis, up)
        after = lax.ppermute(leading, axis, down)
        array = jnp.concatenate([before, array, after], axis=dim)
    return array


def dft_tables(width):
    index = jnp.arange(width)
    product = index[:, None] * index[None, :] % width
    angles = product.astype(jnp.float32) * (2.0 * math.pi / width)
    scale = 1.0 / math.sqrt(width)
    return (jnp.cos(angles) * scale, jnp.sin(angles) * scale)


def left_apply(matrix, field):
    return jnp.einsum("ij,...jk->...ik", matrix, field, precision=exact)


def right_apply(field, matrix):
    return jnp.einsum("...ij,jk->...ik", field, matrix, precision=exact)


def transform(pair, cosine, sine, sign):
    real_part, imag_part = pair
    imag_table = sign * sine
    left_real = left_apply(cosine, real_part) - left_apply(imag_table, imag_part)
    left_imag = left_apply(cosine, imag_part) + left_apply(imag_table, real_part)
    return (
        right_apply(left_real, cosine) - right_apply(left_imag, imag_table),
        right_apply(left_real, imag_table) + right_apply(left_imag, cosine),
    )


def times_complex(first, second):
    return (
        first[0] * second[0] - first[1] * second[1],
        first[0] * second[1] + first[1] * second[0],
    )


def conjugate_times(first, second):
    return (
        first[0] * second[0] + first[1] * second[1],
        first[0] * second[1] - first[1] * second[0],
    )


def window_gradients(windows, amplitude, probe, phase, cosine, sine):
    slices = windows.shape[1] // 2
    layers = [(windows[:, 2 * layer], windows[:, 2 * layer + 1]) for layer in range(slices)]
    probe_pair = (probe[0], probe[1])
    kernel = (jnp.cos(phase), jnp.sin(phase))
    kernel_conj = (kernel[0], -kernel[1])

    def propagate(field, factor):
        spectrum = transform(field, cosine, sine, -1.0)
        return transform(times_complex(factor, spectrum), cosine, sine, 1.0)

    wave = times_complex(probe_pair, layers[0])
    layer = 1
    moved = propagate(wave, kernel)
    incoming = [moved]
    wave = times_complex(layers[layer], moved)
    far_field = transform(wave, cosine, sine, -1.0)
    magnitude = jnp.sqrt(far_field[0] * far_field[0] + far_field[1] * far_field[1] + 1.0)
    factor = 1.0 - amplitude / magnitude
    back = transform((far_field[0] * factor, far_field[1] * factor), cosine, sine, 1.0)
    grads = [None] * slices
    layer = 1
    grads[layer] = conjugate_times(incoming[layer - 1], back)
    back = propagate(conjugate_times(layers[layer], back), kernel_conj)
    grads[0] = conjugate_times(probe_pair, back)
    return jnp.stack([part for pair in grads for part in pair], axis=1)


def slot_table(owner):
    order = jnp.arange(owner.shape[0])
    same = owner[:, None] == owner[None, :]
    earlier = order[None, :] < order[:, None]
    return jnp.sum(jnp.where(same & earlier, 1, 0), axis=1).astype(jnp.int32)


def smooth_padded(padded):
    center = padded[:, 1:-1, 1:-1]
    views = [padded[:, 2:, 1:-1], padded[:, :-2, 1:-1], padded[:, 1:-1, 2:], padded[:, 1:-1, :-2]]
    slices = center.shape[0] // 2
    total = jnp.zeros_like(center)
    for view in views:
        pairs = (view - center).reshape((slices, 2) + center.shape[1:])
        weight = 1.0 / jnp.sqrt(1.0 + pairs[:, 0] * pairs[:, 0] + pairs[:, 1] * pairs[:, 1])
        total = total + (pairs * weight[:, None]).reshape(center.shape)
    return center + smooth_rate * total


def accumulate(total, grads, tops, lefts):
    zero_index = jnp.zeros((), jnp.int32)

    def add_one(index, acc):
        piece = grads[index]
        start = (zero_index, tops[index], lefts[index])
        current = lax.dynamic_slice(acc, start, piece.shape)
        return lax.dynamic_update_slice(acc, current + piece, start)

    return lax.fori_loop(0, grads.shape[0], add_one, total)


def per_device(object_init, probe, propagator_phase, measured, corners, owner_column):
    width = probe.shape[-1]
    cosine, sine = dft_tables(width)
    field = object_init
    channels = field.shape[0]
    columns = lax.axis_size("ty")
    capacity = measured.shape[3]
    tops = corners[0, 0, :, 0]
    lefts = corners[0, 0, :, 1]
    owner = owner_column[0, 0, :, 0]
    slot = slot_table(owner)
    target = owner * capacity + slot
    selector = (jnp.arange(columns * capacity)[:, None] == target[None, :]).astype(jnp.bfloat16)
    local_measured = measured[0, 0]
    zero_index = jnp.zeros((), jnp.int32)
    windows = jax.vmap(
        lambda top, left: lax.dynamic_slice(
            field, (zero_index, top, left), (channels, width, width)
        )
    )(tops, lefts)
    windows = windows.astype(jnp.bfloat16)
    outgoing = jnp.einsum(
        "mk,kcij->mcij", selector, windows, preferred_element_type=jnp.float32
    ).astype(jnp.bfloat16)
    outgoing = outgoing.reshape(columns, capacity, channels, width, width)
    incoming = lax.all_to_all(outgoing, "ty", split_axis=0, concat_axis=0, tiled=True)
    slot_windows = incoming.reshape(columns * capacity, channels, width, width).astype(jnp.float32)
    slot_amplitude = local_measured.reshape(columns * capacity, width, width).astype(jnp.float32)
    slot_grads = window_gradients(
        slot_windows, slot_amplitude, probe, propagator_phase, cosine, sine
    ).astype(jnp.bfloat16)
    returned = lax.all_to_all(
        slot_grads.reshape(columns, capacity, channels, width, width),
        "ty",
        split_axis=0,
        concat_axis=0,
        tiled=True,
    )
    returned = returned.reshape(columns * capacity, channels, width, width)
    grads = jnp.einsum("mk,mcij->kcij", selector, returned, preferred_element_type=jnp.float32)
    total = accumulate(jnp.zeros(field.shape, jnp.float32), grads, tops, lefts)
    updated = field - step_rate * total
    padded = padded_2(updated, (("tx", 1), ("ty", 2)), 1)
    field = smooth_padded(padded)
    return field


def solution(mesh):
    placed = (
        P(None, "tx", "ty"),
        P(),
        P(),
        P("tx", "ty", None, None, None, None),
        P("tx", "ty", None, None),
        P("tx", "ty", None, None),
    )
    return jax.shard_map(
        per_device, mesh=mesh, in_specs=placed, out_specs=P(None, "tx", "ty"), check_vma=False
    )
```

profile of v0, /device:TPU:0, one launch (start us, length us, event | category | flops | bytes accessed | tf_op | source)
XLA Modules:
  0.0 393.1 jit_solution(15614261268332631315)
XLA Ops:
  2.1 35.6 %while.15 = (s32[]{:T(128)}, bf16[4,256,256]{2,1,0:T(8,128)(2,1)S(1)}, s32[16,3]{0,1:T(4,128)S(1)}, bf16[16,4,128,128]{3,2,1,0:T(8,128)(2,1)S(1)}, s32[]{:T(128)}) while((s32[]{:T(128)}, bf16[4,256,256]{2,1,0:T(8,128)(2,1)S(1)}, s32[16,3]{0,1:T(4,128)S(1)}, bf16[16,4,128,128]{3,2,1,0:T(8,128)(2,1)S(1)}, s32[]{:T(128)}) %tuple.66), condition=%wide.while_cond, body=%wide.while_body.sunk | while | flops 2 | bytes 262261 | solution.py:142
  39.4 3.6 copy.247
  42.9 5.4 %all-to-all-start = ((bf16[8,2,4,128,128]{4,1,3,2,0:T(2,128)(2,1)}), bf16[8,2,4,128,128]{4,1,3,2,0:T(2,128)(2,1)S(1)}, u32[]{:S(2)}, u32[]{:S(2)}) async-start(bf16[8,2,4,128,128]{4,1,3,2,0:T(2,128)(2,1)} %copy.247), calls=%async_computation | async-start | bytes 4194304 | tf_op jit(solution)/shard_map/all_to_all | solution.py:151
  48.7 26.2 %all-to-all-done = bf16[8,2,4,128,128]{4,1,3,2,0:T(2,128)(2,1)S(1)} async-done(((bf16[8,2,4,128,128]{4,1,3,2,0:T(2,128)(2,1)}), bf16[8,2,4,128,128]{4,1,3,2,0:T(2,128)(2,1)S(1)}, u32[]{:S(2)}, u32[]{:S(2)}) %all-to-all-start) | async-done | bytes 2097184 | tf_op jit(solution)/shard_map/all_to_all | solution.py:151
  76.1 2.0 fusion.50
  78.1 2.0 fusion.49
  80.1 2.0 fusion.16
  86.1 2.2 fusion.15
  92.2 2.0 fusion.46
  94.2 2.0 fusion.45
  96.2 2.0 fusion.14
  98.3 2.3 fusion.64
  102.5 2.0 fusion.13
  104.6 2.0 convolution_add_fusion.8
  106.6 2.1 multiply_add_fusion.2
  110.6 2.1 fusion.108
  122.6 2.4 fusion.27
  134.7 2.3 fusion.9
  139.1 2.3 multiply_subtract_fusion.2
  147.2 2.1 fusion.92
  157.1 2.0 fusion.48
  159.2 2.2 fusion.47
  161.4 2.0 fusion.6
  167.3 2.0 fusion.5
  171.2 2.3 add_convert_fusion.1
  175.1 3.7 all-to-all-start.1
  178.9 26.6 %all-to-all-done.1 = bf16[8,2,4,128,128]{4,3,1,2,0:T(8,128)(2,1)S(1)} async-done(((bf16[8,2,4,128,128]{4,3,1,2,0:T(8,128)(2,1)}), bf16[8,2,4,128,128]{4,3,1,2,0:T(8,128)(2,1)S(1)}, u32[]{:S(2)}, u32[]{:S(2)}) %all-to-all-start.1) | async-done | bytes 2097184 | tf_op jit(solution)/shard_map/all_to_all | solution.py:157
  205.4 2.2 copy.305
  207.6 2.7 fusion.126
  210.4 165.7 %while.14 = (s32[]{:T(128)}, f32[4,256,256]{2,1,0:T(8,128)S(1)}, s32[16]{0:T(128)S(1)}, s32[16]{0:T(128)S(1)}, f32[16,4,128,128]{3,0,2,1:T(8,128)}, /*index=5*/s32[]{:T(128)}, s32[]{:T(128)}, s32[]{:T(128)}) while((s32[]{:T(128)}, f32[4,256,256]{2,1,0:T(8,128)S(1)}, s32[16]{0:T(128)S(1)}, s32[16]{0:T(128)S(1)}, f32[16,4,128,128]{3,0,2,1:T(8,128)}, ...), condition=%wide.region_2.3_spmd, body=%wide.region_1.2_spmd.sunk | while | flops 65544 | bytes 1835201 | solution.py:123
  217.4 3.1 dynamic_update_slice.8
  227.6 3.2 dynamic_update_slice.8
  237.9 3.4 dynamic_update_slice.8
  248.4 3.0 dynamic_update_slice.8
  258.5 3.4 dynamic_update_slice.8
  269.0 3.4 dynamic_update_slice.8
  279.5 3.3 dynamic_update_slice.8
  289.9 3.2 dynamic_update_slice.8
  300.2 3.3 dynamic_update_slice.8
  310.5 3.3 dynamic_update_slice.8
  320.9 3.2 dynamic_update_slice.8
  331.2 3.3 dynamic_update_slice.8
  341.6 3.4 dynamic_update_slice.8
  352.1 3.4 dynamic_update_slice.8
  362.5 3.1 dynamic_update_slice.8
  372.6 3.4 dynamic_update_slice.8
  377.6 4.5 %collective-permute-start.1 = (f32[4,1,256]{2,1,0:T(1,128)S(1)}, f32[4,1,256]{2,1,0:T(1,128)S(1)}, u32[]{:S(2)}, u32[]{:S(2)}) collective-permute-start(f32[4,1,256]{2,1,0:T(1,128)S(1)} %get-tuple-element.171), channel_id=1, source_target_pairs={{0,8},{8,16},{16,24},{1,9},{9,17},{17,25},{2,10},{10,18},{18,26},{... | collective-permute-start | bytes 12296 | tf_op jit(solution)/shard_map/ppermute | solution.py:20
  385.6 3.0 collective-permute-start.3
  (185 shorter events, 155.4 us)
Async XLA Ops:
  0.0 37.7 %copy-start.5 = (s32[1,1,16,1]{2,3,1,0:T(1,128)S(1)}, s32[1,1,16,1]{2,3,1,0:T(1,128)}, u32[]{:S(2)}) copy-start(s32[1,1,16,1]{2,3,1,0:T(1,128)} %param.13) | copy-start | bytes 196
  42.9 5.5 %copy-start.3 = (f32[128,128]{1,0:T(8,128)S(1)}, f32[128,128]{1,0:T(8,128)}, u32[]{:S(2)}) copy-start(f32[128,128]{1,0:T(8,128)} %param.10) | copy-start | bytes 196612
  42.9 5.7 %copy-start.2 = (f32[2,128,128]{2,1,0:T(8,128)S(1)}, f32[2,128,128]{2,1,0:T(8,128)}, u32[]{:S(2)}) copy-start(f32[2,128,128]{2,1,0:T(8,128)} %param.9) | copy-start | bytes 393220
  42.9 31.9 %all-to-all-start = ((bf16[8,2,4,128,128]{4,1,3,2,0:T(2,128)(2,1)}), bf16[8,2,4,128,128]{4,1,3,2,0:T(2,128)(2,1)S(1)}, u32[]{:S(2)}, u32[]{:S(2)}) async-start(bf16[8,2,4,128,128]{4,1,3,2,0:T(2,128)(2,1)} %copy.247), calls=%async_computation | async-start | bytes 4194304 | tf_op jit(solution)/shard_map/all_to_all | solution.py:151
  120.6 2.0 copy-start.1
  175.1 3.7 copy-start.4
  175.1 30.3 %all-to-all-start.1 = ((bf16[8,2,4,128,128]{4,3,1,2,0:T(8,128)(2,1)}), bf16[8,2,4,128,128]{4,3,1,2,0:T(8,128)(2,1)S(1)}, u32[]{:S(2)}, u32[]{:S(2)}) async-start(bf16[8,2,4,128,128]{4,3,1,2,0:T(8,128)(2,1)} %pad_maximum_fusion), calls=%async_computation.1 | async-start | bytes 4194304 | tf_op jit(solution)/shard_map/all_to_all | solution.py:157
  210.4 165.7 %copy-start = (f32[4,256,256]{2,1,0:T(8,128)S(1)}, f32[4,256,256]{2,1,0:T(8,128)}, u32[]{:S(2)}) copy-start(f32[4,256,256]{2,1,0:T(8,128)} %param.8) | copy-start | bytes 3145732
  376.3 5.9 %collective-permute-start = (f32[4,1,256]{2,1,0:T(1,128)S(1)}, f32[4,1,256]{2,1,0:T(1,128)S(1)}, u32[]{:S(2)}, u32[]{:S(2)}) collective-permute-start(f32[4,1,256]{2,1,0:T(1,128)S(1)} %get-tuple-element.172), channel_id=1, source_target_pairs={{8,0},{16,8},{24,16},{9,1},{17,9},{25,17},{10,2},{18,10},{26,18},{... | collective-permute-start | bytes 12296 | tf_op jit(solution)/shard_map/ppermute | solution.py:21
  377.6 5.9 %collective-permute-start.1 = (f32[4,1,256]{2,1,0:T(1,128)S(1)}, f32[4,1,256]{2,1,0:T(1,128)S(1)}, u32[]{:S(2)}, u32[]{:S(2)}) collective-permute-start(f32[4,1,256]{2,1,0:T(1,128)S(1)} %get-tuple-element.171), channel_id=1, source_target_pairs={{0,8},{8,16},{16,24},{1,9},{9,17},{17,25},{2,10},{10,18},{18,26},{... | collective-permute-start | bytes 12296 | tf_op jit(solution)/shard_map/ppermute | solution.py:20
  384.0 4.6 %collective-permute-start.2 = (f32[4,258,1]{1,0,2:T(4,128)S(1)}, f32[4,258,1]{1,0,2:T(4,128)S(1)}, u32[]{:S(2)}, u32[]{:S(2)}) collective-permute-start(f32[4,258,1]{1,0,2:T(4,128)S(1)} %copy.307), channel_id=1, source_target_pairs={{1,0},{2,1},{3,2},{4,3},{5,4},{6,5},{7,6},{9,8},{10,9},{11,10},{12... | collective-permute-start | bytes 12392 | tf_op jit(solution)/shard_map/ppermute | solution.py:21
  385.6 3.8 collective-permute-start.3
where the time goes:
time: 399 us; the launch traced here: 393 us
  local copies, waits for them, and re-layouts  145 us (36%)
  matrix products  101 us (25%)
  loops' own time  61.8 us (15%)
  waiting for transfers between devices  54.6 us (14%)
  starting transfers between devices  19.3 us (5%)
  other arithmetic  10.1 us (3%)
    another operation x1, loops' own time, accumulate(): return lax.fori_loop(0, grads.shape[0], add_one, total)  61.5 us
    dynamic_update_slice x16, local copies, waits for them, and re-layouts, add_one(): return lax.dynamic_update_slice(acc, current + piece, start)  52.4 us
    dot_general x24, matrix products, right_apply(): return jnp.einsum('...ij,jk->...ik', field, matrix, precision=exact)  48.5 us
    dot_general x24, matrix products, left_apply(): return jnp.einsum('ij,...jk->...ik', matrix, field, precision=exact)  48.5 us
    gather x48, local copies, waits for them, and re-layouts  35.3 us
    dynamic_slice x16, local copies, waits for them, and re-layouts, add_one(): piece = grads[index]  28.5 us
    all_to_all x1, waiting for transfers between devices, per_device(): lax.all_to_all(slot_grads.reshape(columns, capacity, channels, width, wid...  26.6 us
    all_to_all x1, waiting for transfers between devices, per_device(): lax.all_to_all(outgoing, 'ty', split_axis=0, concat_axis=0, tiled=True)  26.2 us
  transfers between devices with their start and end apart: 6, of which 4 were waited for; matrix products, arithmetic and copies ran while one was open for 0% of the time, Pallas kernels for 0%

commit v1 on v0

v1 whole, which is shorter than its diff:
```python
import functools
import math

import jax
import jax.numpy as jnp
import numpy as np
from jax import lax
from jax.experimental import pallas as pl
from jax.experimental.pallas import tpu as pltpu
from jax.sharding import PartitionSpec as P

step_rate = 0.5
smooth_rate = 0.2
group = 4


def dft_blocks(width):
    index = np.arange(width)
    angles = (index[:, None] * index[None, :] % width) * (2.0 * math.pi / width)
    cosine = np.cos(angles) / math.sqrt(width)
    sine = np.sin(angles) / math.sqrt(width)
    blocks = [
        np.block([[cosine, sine], [-sine, cosine]]).astype(np.float32),
        np.block([[cosine, -sine], [sine, cosine]]).astype(np.float32),
    ]
    parts = []
    for block in blocks:
        head = block.astype(jnp.bfloat16)
        parts += [head, (block - head.astype(np.float32)).astype(jnp.bfloat16)]
    return jnp.asarray(np.stack(parts))


def times(a, b):
    return (a[0] * b[0] - a[1] * b[1], a[0] * b[1] + a[1] * b[0])


def conj_times(a, b):
    return (a[0] * b[0] + a[1] * b[1], a[0] * b[1] - a[1] * b[0])


def dot(a, b):
    return jnp.dot(a, b, preferred_element_type=jnp.float32)


def transform_two(first, second, left, right, width):
    field = jnp.concatenate(
        [
            jnp.concatenate([first[0], second[0]], axis=1),
            jnp.concatenate([first[1], second[1]], axis=1),
        ],
        axis=0,
    ).astype(jnp.bfloat16)
    y = (dot(left[0], field) + dot(left[1], field)).astype(jnp.bfloat16)
    turned = jnp.concatenate(
        [
            jnp.concatenate([y[:width, :width], y[width:, :width]], axis=1),
            jnp.concatenate([y[:width, width:], y[width:, width:]], axis=1),
        ],
        axis=0,
    )
    z = dot(turned, right[0]) + dot(turned, right[1])
    return (
        (z[:width, :width], z[:width, width:]),
        (z[width:, :width], z[width:, width:]),
    )


def transform(fields, tables, inverse, width):
    a, b = (tables[0], tables[1]), (tables[2], tables[3])
    left, right = (b, a) if inverse else (a, b)
    out = []
    for i in range(0, len(fields), 2):
        out += transform_two(fields[i], fields[i + 1], left, right, width)
    return out


def forward(step, refs, scratch, width):
    corners, obj, probe, tables = refs
    h_ref, t1_ref, p_ref, inc_ref, far_ref = scratch
    rows = lax.broadcasted_iota(jnp.int32, (width, width), 0)
    cols = lax.broadcasted_iota(jnp.int32, (width, width), 1)
    h = (h_ref[0], h_ref[1])
    t0s, t1s, ps = [], [], []
    for j in range(group):
        k = step * group + j
        top, left = corners[k, 0], corners[k, 1]
        low_r, low_c = rows >= top, cols >= left

        def cells(ch):
            upper = jnp.where(low_c, obj[ch, :width, :width], obj[ch, :width, width:])
            lower = jnp.where(low_c, obj[ch, width:, :width], obj[ch, width:, width:])
            return jnp.where(low_r, upper, lower).astype(jnp.bfloat16).astype(jnp.float32)

        def turned(ch):
            moved = pltpu.roll(probe[ch], lax.rem(top, width), 0)
            return pltpu.roll(moved, lax.rem(left, width), 1)

        t0s.append((cells(0), cells(1)))
        t1s.append((cells(2), cells(3)))
        ps.append((turned(0), turned(1)))
    wave = [times(p, t) for p, t in zip(ps, t0s)]
    spectrum = transform(wave, tables, False, width)
    inc = transform([times(h, s) for s in spectrum], tables, True, width)
    far = transform([times(t, w) for t, w in zip(t1s, inc)], tables, False, width)
    for j in range(group):
        k = step * group + j
        for c in range(2):
            t1_ref[k, c] = t1s[j][c]
            p_ref[k, c] = ps[j][c]
            inc_ref[k, c] = inc[j][c]
            far_ref[k, c] = far[j][c]


def backward(step, entries, amp, tables, scratch, grads, width):
    h_ref, t1_ref, p_ref, inc_ref, far_ref = scratch
    h = (h_ref[0], h_ref[1])
    damped, t1s = [], []
    for j in range(group):
        k = step * group + j
        far = (far_ref[k, 0], far_ref[k, 1])
        value = amp[entries(k)].astype(jnp.float32)
        factor = 1.0 - value * lax.rsqrt(far[0] * far[0] + far[1] * far[1] + 1.0)
        damped.append((far[0] * factor, far[1] * factor))
        t1s.append((t1_ref[k, 0], t1_ref[k, 1]))
    back = transform(damped, tables, True, width)
    for j in range(group):
        k = step * group + j
        g = conj_times((inc_ref[k, 0], inc_ref[k, 1]), back[j])
        grads[k, 2] = g[0].astype(jnp.bfloat16)
        grads[k, 3] = g[1].astype(jnp.bfloat16)
    spectrum = transform(
        [conj_times(t, w) for t, w in zip(t1s, back)], tables, False, width
    )
    back = transform([conj_times(h, s) for s in spectrum], tables, True, width)
    for j in range(group):
        k = step * group + j
        g = conj_times((p_ref[k, 0], p_ref[k, 1]), back[j])
        grads[k, 0] = g[0].astype(jnp.bfloat16)
        grads[k, 1] = g[1].astype(jnp.bfloat16)


def gather_add(block, corners, obj, grads, out, width):
    count, channels = grads.shape[:2]
    start = pl.multiple_of(block * 16, 16)
    rows = lax.broadcasted_iota(jnp.int32, (16, width), 0) + start
    cols = lax.broadcasted_iota(jnp.int32, (16, width), 1)
    totals = [[jnp.zeros((16, width), jnp.float32)] * 4 for _ in range(channels)]
    for k in range(count):
        low_r, low_c = rows >= corners[k, 0], cols >= corners[k, 1]
        for ch in range(channels):
            g = grads[k, ch, pl.ds(start, 16), :].astype(jnp.float32)
            upper = jnp.where(low_r, g, 0.0)
            lower = g - upper
            upper_left = jnp.where(low_c, upper, 0.0)
            lower_left = jnp.where(low_c, lower, 0.0)
            t = totals[ch]
            totals[ch] = [
                t[0] + upper_left,
                t[1] + (upper - upper_left),
                t[2] + lower_left,
                t[3] + (lower - lower_left),
            ]
    for ch in range(channels):
        for part in range(4):
            at = pl.ds(pl.multiple_of(start + (part // 2) * width, 16), 16)
            side = pl.ds((part % 2) * width, width)
            out[ch, at, side] = obj[ch, at, side] - step_rate * totals[ch][part]


def tile_edges(upd, edges):
    channels, size = upd.shape[0], upd.shape[1]
    for ch in range(channels):
        edges[0, ch : ch + 1, :] = upd[ch, 0:1, :]
        edges[1, ch : ch + 1, :] = upd[ch, size - 1 : size, :]
        edges[2, ch : ch + 1, :] = upd[ch, :, 0:128].T[0:1, :]
        edges[3, ch : ch + 1, :] = upd[ch, :, size - 128 :].T[127:128, :]


def smooth(upd, above, below, before, after, out):
    channels, size = upd.shape[0], upd.shape[1]
    rows = lax.broadcasted_iota(jnp.int32, (size, size), 0)
    cols = lax.broadcasted_iota(jnp.int32, (size, size), 1)

    def column(row):
        return jnp.broadcast_to(row, (128, size)).T[:, 0:1]

    for s in range(channels // 2):
        pair = (2 * s, 2 * s + 1)
        v = [upd[ch] for ch in pair]
        up = [jnp.where(rows == 0, above[ch : ch + 1, :], pltpu.roll(x, 1, 0)) for ch, x in zip(pair, v)]
        down = [
            jnp.where(rows == size - 1, below[ch : ch + 1, :], pltpu.roll(x, size - 1, 0))
            for ch, x in zip(pair, v)
        ]
        left = [
            jnp.where(cols == 0, column(before[ch : ch + 1, :]), pltpu.roll(x, 1, 1))
            for ch, x in zip(pair, v)
        ]
        right = [
            jnp.where(cols == size - 1, column(after[ch : ch + 1, :]), pltpu.roll(x, size - 1, 1))
            for ch, x in zip(pair, v)
        ]
        total = [jnp.zeros_like(v[0]), jnp.zeros_like(v[0])]
        for view in (up, down, left, right):
            d = [view[0] - v[0], view[1] - v[1]]
            weight = lax.rsqrt(1.0 + d[0] * d[0] + d[1] * d[1])
            total = [total[0] + d[0] * weight, total[1] + d[1] * weight]
        for ch, x, t in zip(pair, v, total):
            out[ch] = x + smooth_rate * t


def step_kernel(
    corners, owner, obj, probe, phase, table_ref, amp, upd, edges,
    h_ref, t1_ref, p_ref, inc_ref, far_ref, grads,
):
    width, count = probe.shape[-1], corners.shape[0]
    scratch = (h_ref, t1_ref, p_ref, inc_ref, far_ref)
    h_ref[0] = jnp.cos(phase[...])
    h_ref[1] = jnp.sin(phase[...])
    tables = [table_ref.at[i] for i in range(4)]

    def entry(k):
        mine = owner[k]

        def same(i, n):
            return n + jnp.where((owner[i] == mine) & (i < k), 1, 0)

        slot = lax.fori_loop(0, count, same, jnp.int32(0), unroll=True)
        return mine, slot

    @pl.loop(0, count // group)
    def _(step):
        forward(step, (corners, obj, probe, [t[...] for t in tables]), scratch, width)

    @pl.loop(0, count // group)
    def _(step):
        backward(step, entry, amp, [t[...] for t in tables], scratch, grads, width)

    @pl.loop(0, width // 16)
    def _(block):
        gather_add(block, corners, obj, grads, upd, width)

    tile_edges(upd, edges)


def smooth_kernel(upd, above, below, before, after, out):
    smooth(upd, above, below, before, after, out)


def per_device(object_init, probe, propagator_phase, measured, corners, owner_column):
    width = probe.shape[-1]
    channels, size = object_init.shape[0], object_init.shape[1]
    count = corners.shape[2]
    amp = lax.all_to_all(measured[0, 0], "ty", split_axis=0, concat_axis=0, tiled=True)
    smem = pl.BlockSpec(memory_space=pltpu.SMEM)
    vmem = pl.BlockSpec(memory_space=pltpu.VMEM)
    held = pltpu.VMEM((count, 2, width, width), jnp.float32)
    upd, edges = pl.pallas_call(
        step_kernel,
        out_shape=(
            jax.ShapeDtypeStruct(object_init.shape, jnp.float32),
            jax.ShapeDtypeStruct((4, channels, size), jnp.float32),
        ),
        in_specs=[smem, smem] + [vmem] * 5,
        out_specs=(vmem, vmem),
        scratch_shapes=[
            pltpu.VMEM((2, width, width), jnp.float32),
            held, held, held, held,
            pltpu.VMEM((count, channels, width, width), jnp.bfloat16),
        ],
        compiler_params=pltpu.CompilerParams(vmem_limit_bytes=48 * 1024 * 1024),
    )(corners[0, 0], owner_column[0, 0, :, 0], object_init, probe, propagator_phase,
      dft_blocks(width), amp)
    halos = []
    for axis, first, last in (("tx", 0, 1), ("ty", 2, 3)):
        n = lax.axis_size(axis)
        up = [(i, i + 1) for i in range(n - 1)]
        down = [(i + 1, i) for i in range(n - 1)]
        halos.append(lax.ppermute(edges[last], axis, up))
        halos.append(lax.ppermute(edges[first], axis, down))
    return pl.pallas_call(
        smooth_kernel,
        out_shape=jax.ShapeDtypeStruct(object_init.shape, jnp.float32),
        in_specs=[vmem] * 5,
        out_specs=vmem,
        compiler_params=pltpu.CompilerParams(vmem_limit_bytes=48 * 1024 * 1024),
    )(upd, *halos)


def solution(mesh):
    placed = (
        P(None, "tx", "ty"),
        P(),
        P(),
        P("tx", "ty", None, None, None, None),
        P("tx", "ty", None, None),
        P("tx", "ty", None, None),
    )
    return jax.shard_map(
        per_device, mesh=mesh, in_specs=placed, out_specs=P(None, "tx", "ty"), check_vma=False
    )
```

time: 399 us -> 49.7 us (0.12); the launches traced: 393 us -> 49.3 us
  local copies, waits for them, and re-layouts: 145 us -> 3.56 us
  matrix products: 101 us -> 0 us
  loops' own time: 61.8 us -> 0 us
  waiting for transfers between devices: 54.6 us -> 10.3 us
  Pallas kernels: 0 us -> 20 us
  other arithmetic: 10.1 us -> 0 us
    dot_general x50 -> x0, matrix products: 101 us -> none  [the longest x24 48.5 us: right_apply(): return jnp.einsum('...ij,jk->...ik', field, matrix, precision=exact)]
    another operation x2 -> x0, loops' own time: 61.8 us -> none  [the longest x1 61.5 us: accumulate(): return lax.fori_loop(0, grads.shape[0], add_one, total)]
    dynamic_update_slice x16 -> x0, local copies, waits for them, and re-layouts: 52.4 us -> none  [add_one(): return lax.dynamic_update_slice(acc, current + piece, start)]
    dynamic_slice x48 -> x0, local copies, waits for them, and re-layouts: 49.4 us -> none  [the longest x16 28.5 us: add_one(): piece = grads[index]]
    all_to_all x2 -> x1, waiting for transfers between devices: 52.7 us -> 8.98 us  [per_device(): lax.all_to_all(measured[0, 0], 'ty', split_axis=0, concat_axis=0, tiled=T...]
    gather x48 -> x0, local copies, waits for them, and re-layouts: 35.3 us -> none
    pallas_call x0 -> x2, Pallas kernels: none -> 20 us  [the longest x1 17.4 us: per_device(): pl.pallas_call(step_kernel, out_shape=(jax.ShapeDtypeStruct(object_init.s...]
    add x18 -> x0, other arithmetic: 4.25 us -> none  [the longest x16 2.37 us: add_one(): return lax.dynamic_update_slice(acc, current + piece, start)]
  transfers between devices with their start and end apart: 6 -> 5, of which waited for: 4 -> 2; matrix products, arithmetic and copies ran while one was open for 0% -> 0% of each run, Pallas kernels for 0% -> 0%
where the time goes in v1:
time: 49.7 us; the launch traced here: 49.3 us
  Pallas kernels  20 us (40%)
  starting transfers between devices  15.5 us (31%)
  waiting for transfers between devices  10.3 us (21%)
  local copies, waits for them, and re-layouts  3.56 us (7%)
    pallas_call x1, Pallas kernels, per_device(): pl.pallas_call(step_kernel, out_shape=(jax.ShapeDtypeStruct(object_init.s...  17.4 us
    all_to_all x1, waiting for transfers between devices, per_device(): lax.all_to_all(measured[0, 0], 'ty', split_axis=0, concat_axis=0, tiled=T...  8.98 us
    ppermute x2, starting transfers between devices, per_device(): halos.append(lax.ppermute(edges[last], axis, up))  7.58 us
    all_to_all x1, starting transfers between devices, per_device(): lax.all_to_all(measured[0, 0], 'ty', split_axis=0, concat_axis=0, tiled=T...  5.3 us
    unnamed x12, local copies, waits for them, and re-layouts  3.47 us
    ppermute x2, starting transfers between devices, per_device(): halos.append(lax.ppermute(edges[first], axis, down))  2.58 us
    pallas_call x1, Pallas kernels, per_device(): pl.pallas_call(smooth_kernel, out_shape=jax.ShapeDtypeStruct(object_init....  2.58 us
    ppermute x2, waiting for transfers between devices, per_device(): halos.append(lax.ppermute(edges[last], axis, up))  1.28 us
  transfers between devices with their start and end apart: 5, of which 2 were waited for; matrix products, arithmetic and copies ran while one was open for 0% of the time, Pallas kernels for 0%

profile of v1, /device:TPU:0, one launch (start us, length us, event | category | flops | bytes accessed | tf_op | source)
XLA Modules:
  0.0 49.3 jit_solution(8223200057258381673)
XLA Ops:
  0.0 0.0 copy-start
  0.0 5.3 %all-to-all-start = ((bf16[8,2,128,128]{3,2,1,0:T(8,128)(2,1)}), bf16[8,2,128,128]{3,2,1,0:T(8,128)(2,1)S(1)}, u32[]{:S(2)}, u32[]{:S(2)}) async-start(bf16[8,2,128,128]{3,2,1,0:T(8,128)(2,1)} %bitcast.12), calls=%async_computation | async-start | bytes 1048576 | tf_op jit(solution)/shard_map/all_to_all | solution.py:254
  5.3 0.0 copy-start.5
  5.3 0.7 %copy-done.5 = s32[1,1,16,2]{2,3,1,0:T(2,128)S(1)} copy-done((s32[1,1,16,2]{2,3,1,0:T(2,128)S(1)}, s32[1,1,16,2]{2,3,1,0:T(2,128)}, u32[]{:S(2)}) %copy-start.5) | copy-done | bytes 152
  6.0 0.1 copy.8.corners
  6.1 0.0 copy-start.4
  6.1 9.0 %all-to-all-done.amp = bf16[8,2,128,128]{3,2,1,0:T(8,128)(2,1)S(1)} async-done(((bf16[8,2,128,128]{3,2,1,0:T(8,128)(2,1)}), bf16[8,2,128,128]{3,2,1,0:T(8,128)(2,1)S(1)}, u32[]{:S(2)}, u32[]{:S(2)}) %all-to-all-start) | async-done | bytes 524320 | tf_op jit(solution)/shard_map/all_to_all | solution.py:254
  15.1 0.0 copy-done
  15.1 0.0 copy-done.4
  15.1 0.0 copy-start.1
  15.1 1.0 %copy-done.1 = bf16[4,256,256]{2,1,0:T(8,128)(2,1)S(1)} copy-done((bf16[4,256,256]{2,1,0:T(8,128)(2,1)S(1)}, bf16[4,256,256]{2,1,0:T(8,128)(2,1)}, u32[]{:S(2)}) %copy-start.1) | copy-done | bytes 524312
  16.1 0.0 copy-start.2
  16.1 0.9 %copy-done.2 = f32[2,128,128]{2,1,0:T(8,128)S(1)} copy-done((f32[2,128,128]{2,1,0:T(8,128)S(1)}, f32[2,128,128]{2,1,0:T(8,128)}, u32[]{:S(2)}) %copy-start.2) | copy-done | bytes 131096
  17.0 0.0 copy-start.3
  17.0 0.8 %copy-done.3 = f32[128,128]{1,0:T(8,128)S(1)} copy-done((f32[128,128]{1,0:T(8,128)S(1)}, f32[128,128]{1,0:T(8,128)}, u32[]{:S(2)}) %copy-start.3) | copy-done | bytes 65560
  17.8 17.4 %shard_map.73 = (f32[4,256,256]{2,1,0:T(8,128)S(1)}, f32[4,4,256]{2,1,0:T(4,128)S(1)}) custom-call(s32[16,2]{1,0:T(8,128)S(1)} %copy.8.corners, s32[16]{0:T(128)S(1)} %bitcast.11, f32[4,256,256]{2,1,0:T(8,128)S(1)} %copy-done, f32[2,128,128]{2,1,0:T(8,128)S(1)} %copy-done.2, f32[128,128]{1,0:T(8,128)S(1)} %copy-done.3, bf16[4,256,256]{2,1,0:T(8,128)(2,1)S(1)} %copy-done.1, ...), custom_call_target="tpu_custom_call" | custom-call | tf_op jit(solution)/shard_map/pallas_call | solution.py:258
  35.3 1.3 %collective-permute-start.3 = (f32[4,256]{1,0:T(4,128)S(1)}, f32[4,256]{1,0:T(4,128)S(1)}, u32[]{:S(2)}, u32[]{:S(2)}) collective-permute-start(f32[4,256]{1,0:T(4,128)S(1)} %get-tuple-element.9), channel_id=1, source_target_pairs={{1,0},{2,1},{3,2},{4,3},{5,4},{6,5},{7,6},{9,8},{10,9},{11,10},{12... | collective-permute-start | bytes 12296 | tf_op jit(solution)/shard_map/ppermute | solution.py:280
  36.6 3.0 %collective-permute-start.2 = (f32[4,256]{1,0:T(4,128)S(1)}, f32[4,256]{1,0:T(4,128)S(1)}, u32[]{:S(2)}, u32[]{:S(2)}) collective-permute-start(f32[4,256]{1,0:T(4,128)S(1)} %get-tuple-element.10), channel_id=1, source_target_pairs={{0,1},{1,2},{2,3},{3,4},{4,5},{5,6},{6,7},{8,9},{9,10},{10,11},{11... | collective-permute-start | bytes 12296 | tf_op jit(solution)/shard_map/ppermute | solution.py:279
  39.6 1.3 %collective-permute-start.1 = (f32[4,256]{1,0:T(4,128)S(1)}, f32[4,256]{1,0:T(4,128)S(1)}, u32[]{:S(2)}, u32[]{:S(2)}) collective-permute-start(f32[4,256]{1,0:T(4,128)S(1)} %get-tuple-element.11), channel_id=1, source_target_pairs={{8,0},{16,8},{24,16},{9,1},{17,9},{25,17},{10,2},{18,10},{26,18},{... | collective-permute-start | bytes 12296 | tf_op jit(solution)/shard_map/ppermute | solution.py:280
  40.9 4.5 %collective-permute-start = (f32[4,256]{1,0:T(4,128)S(1)}, f32[4,256]{1,0:T(4,128)S(1)}, u32[]{:S(2)}, u32[]{:S(2)}) collective-permute-start(f32[4,256]{1,0:T(4,128)S(1)} %get-tuple-element.12), channel_id=1, source_target_pairs={{0,8},{8,16},{16,24},{1,9},{9,17},{17,25},{2,10},{10,18},{18,26},{... | collective-permute-start | bytes 12296 | tf_op jit(solution)/shard_map/ppermute | solution.py:279
  45.5 0.0 collective-permute-done.3.after
  45.5 0.0 collective-permute-done.2.before
  45.5 0.0 collective-permute-done.1.below
  45.5 1.3 %collective-permute-done.above = f32[4,256]{1,0:T(4,128)S(1)} collective-permute-done((f32[4,256]{1,0:T(4,128)S(1)}, f32[4,256]{1,0:T(4,128)S(1)}, u32[]{:S(2)}, u32[]{:S(2)}) %collective-permute-start) | collective-permute-done | bytes 4128 | tf_op jit(solution)/shard_map/ppermute | solution.py:279
  46.8 2.6 %shard_map.74 = f32[4,256,256]{2,1,0:T(8,128)} custom-call(f32[4,256,256]{2,1,0:T(8,128)S(1)} %get-tuple-element.7.upd, f32[4,256]{1,0:T(4,128)S(1)} %collective-permute-done.above, f32[4,256]{1,0:T(4,128)S(1)} %collective-permute-done.1.below, f32[4,256]{1,0:T(4,128)S(1)} %collective-permute-done.2.before, f32[4,256]{1,0:T(4,128)S(1)} %collective-permute-done.3.after), custom_call_target="tpu_custom_call" | custom-call | tf_op jit(solution)/shard_map/pallas_call | solution.py:281
  (1 shorter events, 0.0 us)
Async XLA Ops:
  0.0 15.1 %copy-start = (f32[4,256,256]{2,1,0:T(8,128)S(1)}, f32[4,256,256]{2,1,0:T(8,128)}, u32[]{:S(2)}) copy-start(f32[4,256,256]{2,1,0:T(8,128)} %obj.1) | copy-start | bytes 3145732
  0.0 15.0 %all-to-all-start = ((bf16[8,2,128,128]{3,2,1,0:T(8,128)(2,1)}), bf16[8,2,128,128]{3,2,1,0:T(8,128)(2,1)S(1)}, u32[]{:S(2)}, u32[]{:S(2)}) async-start(bf16[8,2,128,128]{3,2,1,0:T(8,128)(2,1)} %bitcast.12), calls=%async_computation | async-start | bytes 1048576 | tf_op jit(solution)/shard_map/all_to_all | solution.py:254
  5.3 0.7 %copy-start.5 = (s32[1,1,16,2]{2,3,1,0:T(2,128)S(1)}, s32[1,1,16,2]{2,3,1,0:T(2,128)}, u32[]{:S(2)}) copy-start(s32[1,1,16,2]{2,3,1,0:T(2,128)} %param.11) | copy-start | bytes 388
  6.1 9.0 %copy-start.4 = (s32[1,1,16,1]{2,3,1,0:T(1,128)S(1)}, s32[1,1,16,1]{2,3,1,0:T(1,128)}, u32[]{:S(2)}) copy-start(s32[1,1,16,1]{2,3,1,0:T(1,128)} %param.12) | copy-start | bytes 196
  15.1 1.0 %copy-start.1 = (bf16[4,256,256]{2,1,0:T(8,128)(2,1)S(1)}, bf16[4,256,256]{2,1,0:T(8,128)(2,1)}, u32[]{:S(2)}) copy-start(bf16[4,256,256]{2,1,0:T(8,128)(2,1)} %constant.2.clone.table_ref) | copy-start | bytes 1572868
  16.1 0.9 %copy-start.2 = (f32[2,128,128]{2,1,0:T(8,128)S(1)}, f32[2,128,128]{2,1,0:T(8,128)}, u32[]{:S(2)}) copy-start(f32[2,128,128]{2,1,0:T(8,128)} %probe.1) | copy-start | bytes 393220
  17.0 0.8 %copy-start.3 = (f32[128,128]{1,0:T(8,128)S(1)}, f32[128,128]{1,0:T(8,128)}, u32[]{:S(2)}) copy-start(f32[128,128]{1,0:T(8,128)} %phase.1) | copy-start | bytes 196612
  35.3 10.2 %collective-permute-start.3 = (f32[4,256]{1,0:T(4,128)S(1)}, f32[4,256]{1,0:T(4,128)S(1)}, u32[]{:S(2)}, u32[]{:S(2)}) collective-permute-start(f32[4,256]{1,0:T(4,128)S(1)} %get-tuple-element.9), channel_id=1, source_target_pairs={{1,0},{2,1},{3,2},{4,3},{5,4},{6,5},{7,6},{9,8},{10,9},{11,10},{12... | collective-permute-start | bytes 12296 | tf_op jit(solution)/shard_map/ppermute | solution.py:280
  36.6 8.9 %collective-permute-start.2 = (f32[4,256]{1,0:T(4,128)S(1)}, f32[4,256]{1,0:T(4,128)S(1)}, u32[]{:S(2)}, u32[]{:S(2)}) collective-permute-start(f32[4,256]{1,0:T(4,128)S(1)} %get-tuple-element.10), channel_id=1, source_target_pairs={{0,1},{1,2},{2,3},{3,4},{4,5},{5,6},{6,7},{8,9},{9,10},{10,11},{11... | collective-permute-start | bytes 12296 | tf_op jit(solution)/shard_map/ppermute | solution.py:279
  39.6 5.9 %collective-permute-start.1 = (f32[4,256]{1,0:T(4,128)S(1)}, f32[4,256]{1,0:T(4,128)S(1)}, u32[]{:S(2)}, u32[]{:S(2)}) collective-permute-start(f32[4,256]{1,0:T(4,128)S(1)} %get-tuple-element.11), channel_id=1, source_target_pairs={{8,0},{16,8},{24,16},{9,1},{17,9},{25,17},{10,2},{18,10},{26,18},{... | collective-permute-start | bytes 12296 | tf_op jit(solution)/shard_map/ppermute | solution.py:280
  40.9 5.9 %collective-permute-start = (f32[4,256]{1,0:T(4,128)S(1)}, f32[4,256]{1,0:T(4,128)S(1)}, u32[]{:S(2)}, u32[]{:S(2)}) collective-permute-start(f32[4,256]{1,0:T(4,128)S(1)} %get-tuple-element.12), channel_id=1, source_target_pairs={{0,8},{8,16},{16,24},{1,9},{9,17},{17,25},{2,10},{10,18},{18,26},{... | collective-permute-start | bytes 12296 | tf_op jit(solution)/shard_map/ppermute | solution.py:279

commit v2 on v1

--- a/solution.py
+++ b/solution.py
@@ -1,4 +1,3 @@
-import functools
 import math
 
 import jax
@@ -11,6 +10,7 @@
 
 step_rate = 0.5
 smooth_rate = 0.2
+MESH = pl.DeviceIdType.MESH
 group = 4
 
 
@@ -83,7 +83,7 @@
     t0s, t1s, ps = [], [], []
     for j in range(group):
         k = step * group + j
-        top, left = corners[k, 0], corners[k, 1]
+        top, left = corners[0, k], corners[1, k]
         low_r, low_c = rows >= top, cols >= left
 
         def cells(ch):
@@ -146,7 +146,7 @@
     cols = lax.broadcasted_iota(jnp.int32, (16, width), 1)
     totals = [[jnp.zeros((16, width), jnp.float32)] * 4 for _ in range(channels)]
     for k in range(count):
-        low_r, low_c = rows >= corners[k, 0], cols >= corners[k, 1]
+        low_r, low_c = rows >= corners[0, k], cols >= corners[1, k]
         for ch in range(channels):
             g = grads[k, ch, pl.ds(start, 16), :].astype(jnp.float32)
             upper = jnp.where(low_r, g, 0.0)
@@ -210,13 +210,54 @@
 
 
 def step_kernel(
-    corners, owner, obj, probe, phase, table_ref, amp, upd, edges,
+    corners, owner, obj_hbm, probe, phase, table_hbm, measured, out,
+    obj, table_ref, amp, upd, edges, halos,
     h_ref, t1_ref, p_ref, inc_ref, far_ref, grads,
+    local_sem, send_sem, recv_sem, edge_send, edge_recv,
 ):
-    width, count = probe.shape[-1], corners.shape[0]
-    scratch = (h_ref, t1_ref, p_ref, inc_ref, far_ref)
+    width, count = probe.shape[-1], corners.shape[1]
+    columns = measured.shape[0]
+    tx, ty = lax.axis_index("tx"), lax.axis_index("ty")
+    tile_rows = lax.axis_size("tx")
+
+    load_obj = pltpu.make_async_copy(obj_hbm, obj, local_sem.at[0])
+    load_table = pltpu.make_async_copy(table_hbm, table_ref, local_sem.at[1])
+    load_own = pltpu.make_async_copy(measured.at[ty], amp.at[ty], local_sem.at[2])
+    load_obj.start()
+    load_table.start()
+    load_own.start()
+
+    barrier = pltpu.get_barrier_semaphore()
+    for d in range(1, columns):
+        pl.semaphore_signal(
+            barrier, inc=1, device_id={"ty": lax.rem(ty + d, columns)}, device_id_type=MESH
+        )
+    for d in (1, tile_rows - 1):
+        pl.semaphore_signal(
+            barrier, inc=1, device_id={"tx": lax.rem(tx + d, tile_rows)}, device_id_type=MESH
+        )
     h_ref[0] = jnp.cos(phase[...])
     h_ref[1] = jnp.sin(phase[...])
+    pl.semaphore_wait(barrier, columns + 1)
+
+    sends = []
+    for d in range(1, columns):
+        peer = lax.rem(ty + d, columns)
+        sends.append(
+            pltpu.make_async_remote_copy(
+                src_ref=measured.at[peer],
+                dst_ref=amp.at[ty],
+                send_sem=send_sem.at[d - 1],
+                recv_sem=recv_sem.at[d - 1],
+                device_id={"ty": peer},
+                device_id_type=MESH,
+            )
+        )
+    for send in sends:
+        send.start()
+    load_obj.wait()
+    load_table.wait()
+    scratch = (h_ref, t1_ref, p_ref, inc_ref, far_ref)
     tables = [table_ref.at[i] for i in range(4)]
 
     def entry(k):
@@ -226,12 +267,16 @@
             return n + jnp.where((owner[i] == mine) & (i < k), 1, 0)
 
         slot = lax.fori_loop(0, count, same, jnp.int32(0), unroll=True)
-        return mine, slot
+        return mine, jnp.minimum(slot, amp.shape[1] - 1)
 
     @pl.loop(0, count // group)
     def _(step):
         forward(step, (corners, obj, probe, [t[...] for t in tables]), scratch, width)
 
+    load_own.wait()
+    for send in sends:
+        send.wait()
+
     @pl.loop(0, count // group)
     def _(step):
         backward(step, entry, amp, [t[...] for t in tables], scratch, grads, width)
@@ -241,50 +286,66 @@
         gather_add(block, corners, obj, grads, upd, width)
 
     tile_edges(upd, edges)
-
-
-def smooth_kernel(upd, above, below, before, after, out):
-    smooth(upd, above, below, before, after, out)
+    moves = []
+    for source, slot, device in (
+        (1, 0, {"tx": lax.rem(tx + 1, tile_rows)}),
+        (0, 1, {"tx": lax.rem(tx + tile_rows - 1, tile_rows)}),
+        (3, 2, {"ty": lax.rem(ty + 1, columns)}),
+        (2, 3, {"ty": lax.rem(ty + columns - 1, columns)}),
+    ):
+        moves.append(
+            pltpu.make_async_remote_copy(
+                src_ref=edges.at[source],
+                dst_ref=halos.at[slot],
+                send_sem=edge_send.at[slot],
+                recv_sem=edge_recv.at[slot],
+                device_id=device,
+                device_id_type=MESH,
+            )
+        )
+    for move in moves:
+        move.start()
+    for move in moves:
+        move.wait()
+    ends = (tx == 0, tx == tile_rows - 1, ty == 0, ty == columns - 1)
+    smooth(upd, *[jnp.where(end, 0.0, halos[i]) for i, end in enumerate(ends)], out)
 
 
 def per_device(object_init, probe, propagator_phase, measured, corners, owner_column):
     width = probe.shape[-1]
     channels, size = object_init.shape[0], object_init.shape[1]
     count = corners.shape[2]
-    amp = lax.all_to_all(measured[0, 0], "ty", split_axis=0, concat_axis=0, tiled=True)
+    columns = measured.shape[2]
     smem = pl.BlockSpec(memory_space=pltpu.SMEM)
     vmem = pl.BlockSpec(memory_space=pltpu.VMEM)
+    anywhere = pl.BlockSpec(memory_space=pl.ANY)
     held = pltpu.VMEM((count, 2, width, width), jnp.float32)
-    upd, edges = pl.pallas_call(
+    tile = pltpu.VMEM((channels, size, size), jnp.float32)
+    edge = pltpu.VMEM((4, channels, size), jnp.float32)
+    return pl.pallas_call(
         step_kernel,
-        out_shape=(
-            jax.ShapeDtypeStruct(object_init.shape, jnp.float32),
-            jax.ShapeDtypeStruct((4, channels, size), jnp.float32),
-        ),
-        in_specs=[smem, smem] + [vmem] * 5,
-        out_specs=(vmem, vmem),
+        out_shape=jax.ShapeDtypeStruct(object_init.shape, jnp.float32),
+        in_specs=[smem, smem, anywhere, vmem, vmem, anywhere, anywhere],
+        out_specs=vmem,
         scratch_shapes=[
+            tile,
+            pltpu.VMEM((4, 2 * width, 2 * width), jnp.bfloat16),
+            pltpu.VMEM(measured.shape[2:], jnp.bfloat16),
+            tile, edge, edge,
             pltpu.VMEM((2, width, width), jnp.float32),
             held, held, held, held,
             pltpu.VMEM((count, channels, width, width), jnp.bfloat16),
+            pltpu.SemaphoreType.DMA((3,)),
+            pltpu.SemaphoreType.DMA((columns - 1,)),
+            pltpu.SemaphoreType.DMA((columns - 1,)),
+            pltpu.SemaphoreType.DMA((4,)),
+            pltpu.SemaphoreType.DMA((4,)),
         ],
-        compiler_params=pltpu.CompilerParams(vmem_limit_bytes=48 * 1024 * 1024),
-    )(corners[0, 0], owner_column[0, 0, :, 0], object_init, probe, propagator_phase,
-      dft_blocks(width), amp)
-    halos = []
-    for axis, first, last in (("tx", 0, 1), ("ty", 2, 3)):
-        n = lax.axis_size(axis)
-        up = [(i, i + 1) for i in range(n - 1)]
-        down = [(i + 1, i) for i in range(n - 1)]
-        halos.append(lax.ppermute(edges[last], axis, up))
-        halos.append(lax.ppermute(edges[first], axis, down))
-    return pl.pallas_call(
-        smooth_kernel,
-        out_shape=jax.ShapeDtypeStruct(object_init.shape, jnp.float32),
-        in_specs=[vmem] * 5,
-        out_specs=vmem,
-        compiler_params=pltpu.CompilerParams(vmem_limit_bytes=48 * 1024 * 1024),
-    )(upd, *halos)
+        compiler_params=pltpu.CompilerParams(
+            collective_id=0, has_side_effects=True, vmem_limit_bytes=60 * 1024 * 1024
+        ),
+    )(corners[0, 0].T, owner_column[0, 0, :, 0], object_init, probe, propagator_phase,
+      dft_blocks(width), measured[0, 0])
 
 
 def solution(mesh):

time: 49.7 us -> 31.6 us (0.64)
  starting transfers between devices: 15.5 us -> 0 us
  waiting for transfers between devices: 10.3 us -> 0 us
  Pallas kernels: 20 us -> 29.1 us
  local copies, waits for them, and re-layouts: 3.56 us -> 2.29 us
    ppermute x4 -> x0, starting transfers between devices: 10.2 us -> none  [the longest x2 7.58 us: per_device(): halos.append(lax.ppermute(edges[last], axis, up))]
    pallas_call x2 -> x1, Pallas kernels: 20 us -> 29.1 us  [per_device(): pl.pallas_call(step_kernel, out_shape=jax.ShapeDtypeStruct(object_init.sh...]
    all_to_all x1 -> x0, waiting for transfers between devices: 8.98 us -> none  [per_device(): lax.all_to_all(measured[0, 0], 'ty', split_axis=0, concat_axis=0, tiled=T...]
    all_to_all x1 -> x0, starting transfers between devices: 5.3 us -> none  [per_device(): lax.all_to_all(measured[0, 0], 'ty', split_axis=0, concat_axis=0, tiled=T...]
    ppermute x4 -> x0, waiting for transfers between devices: 1.29 us -> none  [the longest x2 1.28 us: per_device(): halos.append(lax.ppermute(edges[last], axis, up))]
    unnamed x12 -> x1, local copies, waits for them, and re-layouts: 3.47 us -> 2.29 us
  transfers between devices with their start and end apart: 5 -> 0, of which waited for: 2 -> 0; matrix products, arithmetic and copies ran while one was open for 0% -> 0% of each run, Pallas kernels for 0% -> 0%
where the time goes in v2:
time: 31.6 us; the launch traced here: 31.4 us
  Pallas kernels  29.1 us (92%)
  local copies, waits for them, and re-layouts  2.29 us (7%)
    pallas_call x1, Pallas kernels, per_device(): pl.pallas_call(step_kernel, out_shape=jax.ShapeDtypeStruct(object_init.sh...  29.1 us
    unnamed x1, local copies, waits for them, and re-layouts  2.29 us

profile of v2, /device:TPU:0, one launch (start us, length us, event | category | flops | bytes accessed | tf_op | source)
XLA Modules:
  0.0 31.4 jit_solution(18303446660484560420)
XLA Ops:
  0.0 29.1 %shard_map.73 = f32[4,256,256]{2,1,0:T(8,128)} custom-call(s32[2,16]{1,0:T(2,128)} %bitcast.6, s32[16]{0:T(128)} %bitcast.7, f32[4,256,256]{2,1,0:T(8,128)} %obj_hbm.1, f32[2,128,128]{2,1,0:T(8,128)} %probe.1, f32[128,128]{1,0:T(8,128)} %phase.1, bf16[4,256,256]{2,1,0:T(8,128)(2,1)} %constant.2.clone.table_hbm, bf16[8,2,128,128]{3,2,1,0:T(8,128)(2,1)} %bitcast.5), custom_call_target="tpu_custom_call" | custom-call | tf_op jit(solution)/shard_map/pallas_call | solution.py:325
  29.1 2.3 %copy.9 = f32[4,256,256]{2,1,0:T(8,128)} copy(f32[4,256,256]{2,1,0:T(8,128)} %shard_map.73) | data formatting | bytes 2097152

commit v3 on v2

--- a/solution.py
+++ b/solution.py
@@ -11,7 +11,7 @@
 step_rate = 0.5
 smooth_rate = 0.2
 MESH = pl.DeviceIdType.MESH
-group = 4
+group = 8
 
 
 def dft_blocks(width):

time: 31.6 us -> 28.1 us (0.89)
  Pallas kernels: 29.1 us -> 25.6 us
    pallas_call x1, Pallas kernels: 29.1 us -> 25.6 us  [per_device(): pl.pallas_call(step_kernel, out_shape=jax.ShapeDtypeStruct(object_init.sh...]
where the time goes in v3:
time: 28.1 us; the launch traced here: 27.9 us
  Pallas kernels  25.6 us (91%)
  local copies, waits for them, and re-layouts  2.29 us (8%)
    pallas_call x1, Pallas kernels, per_device(): pl.pallas_call(step_kernel, out_shape=jax.ShapeDtypeStruct(object_init.sh...  25.6 us
    unnamed x1, local copies, waits for them, and re-layouts  2.29 us

profile of v3, /device:TPU:0, one launch (start us, length us, event | category | flops | bytes accessed | tf_op | source)
XLA Modules:
  0.0 27.9 jit_solution(4149667002924526270)
XLA Ops:
  0.0 25.6 %shard_map.73 = f32[4,256,256]{2,1,0:T(8,128)} custom-call(s32[2,16]{1,0:T(2,128)} %bitcast.6, s32[16]{0:T(128)} %bitcast.7, f32[4,256,256]{2,1,0:T(8,128)} %obj_hbm.1, f32[2,128,128]{2,1,0:T(8,128)} %probe.1, f32[128,128]{1,0:T(8,128)} %phase.1, bf16[4,256,256]{2,1,0:T(8,128)(2,1)} %constant.2.clone.table_hbm, bf16[8,2,128,128]{3,2,1,0:T(8,128)(2,1)} %bitcast.5), custom_call_target="tpu_custom_call" | custom-call | tf_op jit(solution)/shard_map/pallas_call | solution.py:325
  25.6 2.3 %copy.9 = f32[4,256,256]{2,1,0:T(8,128)} copy(f32[4,256,256]{2,1,0:T(8,128)} %shard_map.73) | data formatting | bytes 2097152

commit v4 on v3

--- a/solution.py
+++ b/solution.py
@@ -227,6 +227,7 @@
     load_table.start()
     load_own.start()
 
+    halos[...] = jnp.zeros_like(halos)
     barrier = pltpu.get_barrier_semaphore()
     for d in range(1, columns):
         pl.semaphore_signal(
@@ -287,28 +288,29 @@
 
     tile_edges(upd, edges)
     moves = []
-    for source, slot, device in (
-        (1, 0, {"tx": lax.rem(tx + 1, tile_rows)}),
-        (0, 1, {"tx": lax.rem(tx + tile_rows - 1, tile_rows)}),
-        (3, 2, {"ty": lax.rem(ty + 1, columns)}),
-        (2, 3, {"ty": lax.rem(ty + columns - 1, columns)}),
+    for source, slot, axis, here, size, hop in (
+        (1, 0, "tx", tx, tile_rows, 1),
+        (0, 1, "tx", tx, tile_rows, -1),
+        (3, 2, "ty", ty, columns, 1),
+        (2, 3, "ty", ty, columns, -1),
     ):
-        moves.append(
-            pltpu.make_async_remote_copy(
-                src_ref=edges.at[source],
-                dst_ref=halos.at[slot],
-                send_sem=edge_send.at[slot],
-                recv_sem=edge_recv.at[slot],
-                device_id=device,
-                device_id_type=MESH,
-            )
+        move = pltpu.make_async_remote_copy(
+            src_ref=edges.at[source],
+            dst_ref=halos.at[slot],
+            send_sem=edge_send.at[slot],
+            recv_sem=edge_recv.at[slot],
+            device_id={axis: lax.rem(here + hop + size, size)},
+            device_id_type=MESH,
         )
-    for move in moves:
-        move.start()
-    for move in moves:
-        move.wait()
-    ends = (tx == 0, tx == tile_rows - 1, ty == 0, ty == columns - 1)
-    smooth(upd, *[jnp.where(end, 0.0, halos[i]) for i, end in enumerate(ends)], out)
+        first, last = here == 0, here == size - 1
+        at_end, at_start = (last, first) if hop == 1 else (first, last)
+        moves.append((move, jnp.logical_not(at_end), jnp.logical_not(at_start)))
+    for move, sends_on, _ in moves:
+        pl.when(sends_on)(move.start)
+    for move, sends_on, receives in moves:
+        pl.when(sends_on)(move.wait_send)
+        pl.when(receives)(move.wait_recv)
+    smooth(upd, halos[0], halos[1], halos[2], halos[3], out)
 
 
 def per_device(object_init, probe, propagator_phase, measured, corners, owner_column):

time: 28.1 us -> 27 us (0.961)
  the two profiles are of different devices: /device:TPU:0 before, /device:TPU:1 now
where the time goes in v4:
time: 27 us; the launch traced here: 26.9 us
  Pallas kernels  24.6 us (91%)
  local copies, waits for them, and re-layouts  2.29 us (8%)
    pallas_call x1, Pallas kernels, per_device(): pl.pallas_call(step_kernel, out_shape=jax.ShapeDtypeStruct(object_init.sh...  24.6 us
    unnamed x1, local copies, waits for them, and re-layouts  2.29 us

profile of v4, /device:TPU:1, one launch (start us, length us, event | category | flops | bytes accessed | tf_op | source)
XLA Modules:
  0.0 26.9 jit_solution(16265383779296257072)
XLA Ops:
  0.0 24.6 %shard_map.73 = f32[4,256,256]{2,1,0:T(8,128)} custom-call(s32[2,16]{1,0:T(2,128)} %bitcast.6, s32[16]{0:T(128)} %bitcast.7, f32[4,256,256]{2,1,0:T(8,128)} %obj_hbm.1, f32[2,128,128]{2,1,0:T(8,128)} %probe.1, f32[128,128]{1,0:T(8,128)} %phase.1, bf16[4,256,256]{2,1,0:T(8,128)(2,1)} %constant.2.clone.table_hbm, bf16[8,2,128,128]{3,2,1,0:T(8,128)(2,1)} %bitcast.5), custom_call_target="tpu_custom_call" | custom-call | tf_op jit(solution)/shard_map/pallas_call | solution.py:327
  24.6 2.3 %copy.9 = f32[4,256,256]{2,1,0:T(8,128)} copy(f32[4,256,256]{2,1,0:T(8,128)} %shard_map.73) | data formatting | bytes 2097152
